TPU v7x, 32 devices: a whole 2x2x4 slice. The times are simulated.
32 devices in a mesh: group: 2 (over core), shard: 16 (over z, y, x).
Axes of the slice: x: 2, y: 2, z: 4, core: 2. Of those that a mesh axis runs over, the one named last changes fastest.
Arguments:
- latents: bfloat16 [64, 32, 32, 320], P(('group', 'shard')), may hold values from -6 to 6
- cotangent: bfloat16 [64, 32, 32, 320], P(('group', 'shard')), may hold values from -6 to 6
- weights: float32 [2, 2880, 320], P('group', 'shard'), may hold values from -0.109375 to 0.109375
- momentum: float32 [2, 2880, 320], P('group', 'shard'), may hold values from -6 to 6
- step: int32 [1], replicated, may hold values from 0 to 63
Outputs:
- activations: float32 [64, 32, 32, 320], P(('group', 'shard'))
- data_grad: float32 [64, 32, 32, 320], P(('group', 'shard'))
- new_weights: float32 [2, 2880, 320], P('group', 'shard')
- new_momentum: float32 [2, 2880, 320], P('group', 'shard')
Inputs may be any that keep to these rules, and one draw needn't show every extreme that they name: `step`: one value shared by all devices.
All inputs are finite; a program needn't handle non-finite values.
Results may differ from a plain program's by a relative error of at most 0.0029.
Values may be sent and summed in bfloat16 or wider, within the bound.
A program may use at most 128 MiB of HBM per device.

v0:
```python
from functools import partial

import jax
import jax.numpy as jnp
from jax import lax
from jax.sharding import PartitionSpec as P

beta_rate = 0.9
peak_rate = 0.1
warm_steps = 64.0
tap_offsets = [(row_off, col_off) for row_off in (-1, 0, 1) for col_off in (-1, 0, 1)]


def from_partner(value, axis, bit):
    mask = 2**bit
    pairs = [(source, source ^ mask) for source in range(lax.axis_size(axis))]
    return lax.ppermute(value, axis, pairs)


def shifted_view(padded, row_off, col_off):
    height = padded.shape[1] - 2
    width = padded.shape[2] - 2
    return padded[:, 1 + row_off : 1 + row_off + height, 1 + col_off : 1 + col_off + width, :]


def conv_step(latents, cotangent, kernel):
    channels = kernel.shape[1]
    image_shape = latents.shape
    cell_count = image_shape[0] * image_shape[1] * image_shape[2]
    pad_in = jnp.pad(latents, ((0, 0), (1, 1), (1, 1), (0, 0)))
    pad_co = jnp.pad(cotangent, ((0, 0), (1, 1), (1, 1), (0, 0)))
    flat_co = cotangent.reshape(cell_count, channels)
    forward = jnp.zeros((cell_count, channels), jnp.float32)
    backward = jnp.zeros((cell_count, channels), jnp.float32)
    tap_grads = []
    for tap_index, (row_off, col_off) in enumerate(tap_offsets):
        tap_kernel = kernel[tap_index * channels : (tap_index + 1) * channels]
        moved_in = shifted_view(pad_in, row_off, col_off).reshape(cell_count, channels)
        moved_co = shifted_view(pad_co, -row_off, -col_off).reshape(cell_count, channels)
        forward = forward + jnp.dot(moved_in, tap_kernel, preferred_element_type=jnp.float32)
        backward = backward + lax.dot_general(
            moved_co, tap_kernel, (((1,), (1,)), ((), ())), preferred_element_type=jnp.float32
        )
        tap_grads.append(
            lax.dot_general(
                moved_in, flat_co, (((0,), (0,)), ((), ())), preferred_element_type=jnp.float32
            )
        )
    return (
        forward.reshape(image_shape),
        backward.reshape(image_shape),
        jnp.concatenate(tap_grads, 0),
    )


def trade_pair(payload, level):
    return from_partner(payload, "group", level)


def shards(latents, cotangent, weights, momentum, step):
    kernel_rows = weights[0].astype(jnp.bfloat16)
    kernel = lax.all_gather(kernel_rows, "shard", axis=0, tiled=True)
    forward, backward, partial_grad = conv_step(latents, cotangent, kernel)
    cells_group = lax.axis_size("shard") * latents.shape[0] * latents.shape[1] * latents.shape[2]
    grad_scale = float(cells_group) ** (-0.5)
    learn_rate = peak_rate * (step[0] + 1).astype(jnp.float32) / warm_steps
    shard_rows = weights.shape[1]
    summed = lax.psum(partial_grad, "shard")
    own_rows = lax.dynamic_slice_in_dim(summed, lax.axis_index("shard") * shard_rows, shard_rows, 0)
    moment_new = beta_rate * momentum[0] + own_rows * grad_scale
    updated = weights[0] - learn_rate * moment_new
    bit_count = lax.axis_size("group").bit_length() - 1
    branches = [partial(trade_pair, level=level_index) for level_index in range(bit_count)]
    partner_weights, partner_moment = lax.switch(
        step[0] % bit_count, branches, (updated, moment_new)
    )
    new_weights = (0.5 * (updated + partner_weights))[None]
    new_momentum = (0.5 * (moment_new + partner_moment))[None]
    return (forward, backward, new_weights, new_momentum)


def solution(mesh):
    placed = (
        P(("group", "shard"), None, None, None),
        P(("group", "shard"), None, None, None),
        P("group", "shard", None),
        P("group", "shard", None),
        P(),
    )
    return jax.shard_map(
        shards,
        mesh=mesh,
        in_specs=placed,
        out_specs=(
            P(("group", "shard"), None, None, None),
            P(("group", "shard"), None, None, None),
            P("group", "shard", None),
            P("group", "shard", None),
        ),
        check_vma=False,
    )
```

profile of v0, /device:TPU:0, one launch (start us, length us, event | category | flops | bytes accessed | tf_op | source)
XLA Modules:
  0.0 260.0 jit_solution(5866192705099901427)
XLA Ops:
  7.2 0.0 all-gather.3.cloned.1.call-start
  7.2 1.1 copy.22
  8.3 0.8 copy.23
  9.1 0.0 all-gather.3.cloned.1.call-update
  9.2 0.0 copy-start
  9.2 0.0 copy-start.2
  9.2 0.0 all-reduce.4.cloned.1.call-start
  9.2 3.7 %convolution_bitcast_fusion = f32[320,320]{0,1:T(8,128)} fusion(bf16[2,32,32,320]{3,2,1,0:T(8,128)(2,1)} %param.6, bf16[2,32,32,320]{3,2,1,0:T(8,128)(2,1)} %param.5), kind=kOutput, calls=%fused_computation.32 | convolution fusion | flops 419430400 | bytes 3031040 | tf_op jit(solution)/shard_map/dot_general | solution.py:45
  12.9 1.7 convolution_bitcast_fusion.1
  14.6 1.7 convolution_bitcast_fusion.2
  16.3 1.7 convolution_bitcast_fusion.3
  18.0 1.7 convolution_bitcast_fusion.5
  19.7 1.7 convolution_bitcast_fusion.6
  21.3 1.7 convolution_bitcast_fusion.7
  23.0 1.7 convolution_bitcast_fusion.8
  24.7 1.7 convolution_bitcast_fusion.4
  26.4 5.0 %concatenate.3 = f32[2880,320]{0,1:T(8,128)} concatenate(f32[320,320]{0,1:T(8,128)} %convolution_bitcast_fusion.8, f32[320,320]{0,1:T(8,128)} %convolution_bitcast_fusion.7, f32[320,320]{0,1:T(8,128)} %convolution_bitcast_fusion.6, f32[320,320]{0,1:T(8,128)} %convolution_bitcast_fusion.5, f32[320,320]{0,1:T(8,128)} %convolution_bitcast_fusion.4, ...), dimensions={0} | concatenate | bytes 7372800 | tf_op jit(solution)/shard_map/concatenate | solution.py:52
  31.3 0.0 all-reduce.4.cloned.1.call-update
  31.4 6.4 %pad_slice_fusion = (bf16[2,32,32,320]{3,2,1,0:T(8,128)(2,1)}, bf16[2,32,32,320]{3,2,1,0:T(8,128)(2,1)}, bf16[2,32,32,320]{3,2,1,0:T(8,128)(2,1)}, bf16[2,32,32,...) fusion(bf16[2,32,32,320]{3,2,1,0:T(8,128)(2,1)S(1)} %copy-done), kind=kLoop, calls=%fused_computation.16 | loop fusion | bytes 11796480 | tf_op jit(solution)/shard_map/slice | solution.py:23
  37.8 6.5 %pad_slice_fusion.8 = (bf16[2,32,32,320]{3,2,1,0:T(8,128)(2,1)}, bf16[2,32,32,320]{3,2,1,0:T(8,128)(2,1)}, bf16[2,32,32,320]{3,2,1,0:T(8,128)(2,1)}, bf16[2,32,3...) fusion(bf16[2,32,32,320]{3,2,1,0:T(8,128)(2,1)S(1)} %copy-done.2), kind=kLoop, calls=%fused_computation.24 | loop fusion | bytes 11796480 | tf_op jit(solution)/shard_map/slice | solution.py:23
  44.2 0.2 copy.26
  45.1 31.0 %all-gather.3.cloned.1.call-done = bf16[16,180,320]{2,1,0:T(8,128)(2,1)} async-done(((bf16[1,180,320]{2,1,0:T(8,128)(2,1)}), bf16[16,180,320]{2,1,0:T(8,128)(2,1)}) %all-gather.3.cloned.1.call-update) | async-done | bytes 1843216 | tf_op jit(solution)/shard_map/all_gather | solution.py:62
  76.1 2.8 %reshape.97 = bf16[2880,320]{1,0:T(8,128)(2,1)S(1)} reshape(bf16[16,180,320]{2,1,0:T(8,128)(2,1)} %all-gather.3.cloned.1.call-done) | data formatting | bytes 3686400
  78.9 0.0 copy-start.17
  78.9 2.4 fusion.16
  81.3 0.9 convolution_add_fusion.7
  82.2 0.5 copy-done.16
  82.7 0.9 convolution_add_fusion.6
  83.6 0.5 copy-done.15
  84.1 0.9 convolution_add_fusion.5
  85.0 0.5 copy-done.1
  85.5 0.9 convolution_add_fusion.4
  86.4 0.7 copy-done.14
  87.2 0.9 convolution_add_fusion.3
  88.1 0.5 copy-done.13
  88.6 0.9 convolution_add_fusion.2
  89.5 0.5 copy-done.12
  90.0 0.9 convolution_add_fusion.1
  90.9 0.5 copy-done.11
  91.4 2.4 convolution_add_fusion
  93.8 3.4 %copy.25 = f32[2048,320]{1,0:T(8,128)} copy(f32[2048,320]{0,1:T(8,128)} %convolution_add_fusion) | data formatting | bytes 5242880 | tf_op jit(solution)/shard_map/add | solution.py:41
  97.3 2.4 fusion.18
  99.7 0.9 convolution_add_fusion.15
  100.6 0.5 copy-done.9
  101.1 0.9 convolution_add_fusion.14
  102.0 0.5 copy-done.8
  102.5 0.9 convolution_add_fusion.13
  103.4 0.5 copy-done.3
  104.0 0.9 convolution_add_fusion.12
  104.9 0.5 copy-done.7
  105.4 0.9 convolution_add_fusion.11
  106.3 0.5 copy-done.6
  106.8 0.9 convolution_add_fusion.10
  107.7 0.5 copy-done.5
  108.2 2.4 convolution_add_fusion.9
  110.6 129.5 %all-reduce.4.cloned.1.call-done = f32[2880,320]{0,1:T(8,128)} async-done(((f32[2880,320]{0,1:T(8,128)}), f32[2880,320]{0,1:T(8,128)}) %all-reduce.4.cloned.1.call-update) | async-done | bytes 3686416 | tf_op jit(solution)/shard_map/psum | solution.py:68
  240.1 2.1 bitcast_subtract_fusion
  242.2 0.0 collective-permute-start
  242.2 4.2 %convolution_add_fusion.8 = f32[2048,320]{0,1:T(8,128)} fusion(f32[2048,320]{0,1:T(8,128)} %convolution_add_fusion.9, bf16[2048,320]{1,0:T(8,128)(2,1)S(1)} %bitcast.102, bf16[2880,320]{1,0:T(8,128)(2,1)S(1)} %reshape.97), kind=kOutput, calls=%fused_computation.8 | convolution fusion | flops 420085760 | bytes 7061504 | tf_op jit(solution)/shard_map/dot_general | solution.py:40
  246.4 3.4 %copy.24 = f32[2048,320]{1,0:T(8,128)} copy(f32[2048,320]{0,1:T(8,128)} %convolution_add_fusion.8) | data formatting | bytes 5242880 | tf_op jit(solution)/shard_map/add | solution.py:40
  249.8 0.5 collective-permute-start.1
  250.3 1.0 multiply_bitcast_fusion.1
  251.3 0.9 copy.27
  252.3 0.9 copy.28
  (26 shorter events, 0.1 us)
Async XLA Ops:
  7.2 68.9 %all-gather.3.cloned.1.call-start = ((), (), s32[]{:S(2)}) async-start(), calls=%async_computation.1 | async-start | bytes 2402304 | tf_op jit(solution)/shard_map/all_gather | solution.py:62
  9.2 3.8 %copy-start = (bf16[2,32,32,320]{3,2,1,0:T(8,128)(2,1)S(1)}, bf16[2,32,32,320]{3,2,1,0:T(8,128)(2,1)}, u32[]{:S(2)}) copy-start(bf16[2,32,32,320]{3,2,1,0:T(8,128)(2,1)} %param.6) | copy-start | bytes 3932164
  9.2 3.8 %copy-start.2 = (bf16[2,32,32,320]{3,2,1,0:T(8,128)(2,1)S(1)}, bf16[2,32,32,320]{3,2,1,0:T(8,128)(2,1)}, u32[]{:S(2)}) copy-start(bf16[2,32,32,320]{3,2,1,0:T(8,128)(2,1)} %param.5) | copy-start | bytes 3932164
  9.2 231.0 %all-reduce.4.cloned.1.call-start = ((), (), s32[]{:S(2)}) async-start(), calls=%async_computation | async-start | bytes 7536640 | tf_op jit(solution)/shard_map/psum | solution.py:68
  37.8 6.5 %copy-start.18 = (f32[1,180,320]{2,0,1:T(1,128)S(1)}, f32[1,180,320]{2,0,1:T(1,128)}, u32[]{:S(2)}) copy-start(f32[1,180,320]{2,0,1:T(1,128)} %param.8) | copy-start | bytes 691204
  78.9 2.4 copy-start.17
  81.3 1.4 copy-start.16
  82.7 1.4 copy-start.15
  84.1 1.4 copy-start.1
  85.5 1.7 copy-start.14
  87.2 1.4 copy-start.13
  88.6 1.4 copy-start.12
  90.0 1.4 copy-start.11
  97.2 2.4 copy-start.10
  99.7 1.4 copy-start.9
  101.1 1.4 copy-start.8
  102.5 1.5 copy-start.3
  104.0 1.4 copy-start.7
  105.4 1.4 copy-start.6
  106.8 1.4 copy-start.5
  240.1 2.1 copy-start.4
  242.2 8.1 %collective-permute-start = (f32[180,320]{0,1:T(8,128)}, f32[180,320]{0,1:T(8,128)S(1)}, u32[]{:S(2)}, u32[]{:S(2)}) collective-permute-start(f32[180,320]{0,1:T(8,128)} %get-tuple-element.16), channel_id=1, source_target_pairs={{0,16},{16,0},{1,17},{17,1},{2,18},{18,2},{3,19},{19,3},{4,20},{20... | collective-permute-start | bytes 691208 | tf_op jit(solution)/shard_map/ppermute | solution.py:17
  249.8 2.4 collective-permute-start.1
Sparse Core Ops, SparseCore 0:
  11.3 64.7 all-gather.2
  81.9 158.2 all-reduce.3
where the time goes:
time: 261 us; the launch traced here: 260 us
  waiting for transfers between devices  161 us (62%)
  matrix products  42.7 us (16%)
  local copies, waits for them, and re-layouts  38.1 us (15%)
  between operations  14.9 us (6%)
  other arithmetic  3.14 us (1%)
    psum x1, waiting for transfers between devices, shards(): summed = lax.psum(partial_grad, 'shard')  129 us
    all_gather x1, waiting for transfers between devices, shards(): kernel = lax.all_gather(kernel_rows, 'shard', axis=0, tiled=True)  31 us
    dot_general x9, matrix products, conv_step(): lax.dot_general(moved_in, flat_co, (((0,), (0,)), ((), ())), preferred_el...  17.1 us
    dot_general x9, matrix products, conv_step(): jnp.dot(moved_in, tap_kernel, preferred_element_type=jnp.float32)  14.4 us
    unnamed x44, local copies, waits for them, and re-layouts  13.4 us
    slice x2, local copies, waits for them, and re-layouts, shifted_view(): padded[:, 1 + row_off:1 + row_off + height, 1 + col_off:1 + col_off + wid...  12.9 us
    dot_general x9, matrix products, conv_step(): lax.dot_general(moved_co, tap_kernel, (((1,), (1,)), ((), ())), preferred...  11.1 us
  transfers between devices with their start and end apart: 4, of which 2 were waited for; matrix products, arithmetic and copies ran while one was open for 28% of the time, Pallas kernels for 0%

commit v1 on v0

v1 whole, which is shorter than its diff:
```python
from functools import partial

import jax
import jax.numpy as jnp
from jax import lax
from jax.experimental import pallas as pl
from jax.experimental.pallas import tpu as pltpu
from jax.sharding import PartitionSpec as P

beta_rate = 0.9
peak_rate = 0.1
warm_steps = 64.0
MESH = pl.DeviceIdType.MESH
F32 = jnp.float32
BF16 = jnp.bfloat16
PLANE = 4


def step_kernel(bit, dims, x_ref, c_ref, w_ref, m_ref, step_ref,
                act_ref, dg_ref, nw_ref, nm_ref,
                xc, gc, xt, wg, w32, wf, wb, g32, gb, pr, keep, sb, r1, s2, r2, tot, ptot,
                pw, pm, acc_a, acc_d,
                g_send, g_recv, e_send, e_recv, p_send, p_recv, a_send, a_recv,
                b_send, b_recv, t_send, t_recv, out_sem):
    S, R, RP, C, images, HH, WW = dims
    H = RP // 2
    LN = S // PLANE
    KR = 9 * C
    cells = HH * WW
    pad_cells = cells + 2 * WW
    CP = 384
    grp = lax.axis_index("group")
    me = lax.axis_index("shard")
    q = me // PLANE
    p = me % PLANE
    px = p + 1 - 2 * (p % 2)
    py = (p + 2) % PLANE
    pd = PLANE - 1 - p
    mask = 2 ** bit
    half = (grp // mask) % 2
    mate = grp + mask - 2 * mask * half

    def shard_at(dq, col):
        return ((q + dq) % LN) * PLANE + col

    barrier = pltpu.get_barrier_semaphore()
    peers = [(grp, shard_at(dq, p)) for dq in range(1, LN)]
    peers += [(grp, shard_at(0, col)) for col in (px, py, pd)]
    peers += [(mate, me)]
    for peer in peers:
        pl.semaphore_signal(barrier, inc=1, device_id=peer, device_id_type=MESH)

    wg[me, 0:R, :] = w_ref[...].astype(BF16)
    pl.semaphore_wait(barrier, len(peers))

    started = []

    def send(src, dst, ss, rs, peer):
        copy = pltpu.make_async_remote_copy(src_ref=src, dst_ref=dst, send_sem=ss, recv_sem=rs,
                                            device_id=peer, device_id_type=MESH)
        copy.start()
        started.append(copy)

    def arrived(ref, sem):
        pltpu.make_async_copy(ref, ref, sem).wait()

    g_count = [0]

    def send_piece(slot, peer):
        send(wg.at[slot], wg.at[slot], g_send.at[g_count[0]], g_recv.at[slot], peer)
        g_count[0] += 1

    def wait_piece(slot):
        arrived(wg.at[slot], g_recv.at[slot])

    for dq in range(1, LN):
        send_piece(me, (grp, shard_at(dq, p)))
    x_peer = (grp, shard_at(0, px))
    y_peer = (grp, shard_at(0, py))
    send_piece(me, x_peer)
    send_piece(me, y_peer)
    send(w_ref, pw, e_send.at[0], e_recv.at[0], (mate, me))
    send(m_ref, pm, e_send.at[1], e_recv.at[1], (mate, me))

    def pass_line(dq):
        slot = shard_at(dq, p)
        wait_piece(slot)
        send_piece(slot, x_peer)
        send_piece(slot, y_peer)

    def pass_plane(dq):
        slot_x = shard_at(dq, px)
        slot_y = shard_at(dq, py)
        wait_piece(slot_x)
        wait_piece(slot_y)
        if dq % 2 == 0:
            send_piece(slot_x, y_peer)
        else:
            send_piece(slot_y, x_peer)

    CH = 8 * WW
    for buf in (xc, gc):
        for img in range(images):
            buf[img, 0:WW, :] = jnp.zeros((WW, 3 * CP), BF16)
            buf[img, WW + cells:, :] = jnp.zeros((WW, 3 * CP), BF16)

    def shifted(src, buf, sign):
        def body(k, _):
            img = k // (cells // CH)
            row = (k % (cells // CH)) * CH
            mid = src[pl.ds(pl.multiple_of(k * CH, CH), CH), :]
            val = jnp.concatenate([mid.astype(F32), jnp.zeros((CH, CP - C), F32)], 1)
            col = lax.broadcasted_iota(jnp.int32, (CH, CP), 0) % WW
            prev = jnp.where(col == 0, 0.0, pltpu.roll(val, 1, 0)).astype(BF16)
            nxt = jnp.where(col == WW - 1, 0.0, pltpu.roll(val, CH - 1, 0)).astype(BF16)
            first, last = (prev, nxt) if sign > 0 else (nxt, prev)
            dst = pl.ds(pl.multiple_of(WW + row, WW), CH)
            buf[img, dst, 0:CP] = first
            buf[img, dst, CP:2 * CP] = val.astype(BF16)
            buf[img, dst, 2 * CP:3 * CP] = last
            return 0
        lax.fori_loop(0, images * (cells // CH), body, 0)

    shifted(c_ref, gc, -1)
    for img in range(images):
        xt[img] = x_ref[img * cells:(img + 1) * cells, :].T

    def tap_rows(a):
        total = None
        for img in range(images):
            part = jnp.dot(xt[img], gc[img, WW - WW * (a - 1):WW - WW * (a - 1) + cells, :],
                           preferred_element_type=F32)
            total = part if total is None else total + part
        for b in range(3):
            t = 3 * a + b
            g32[t * C:(t + 1) * C, :] = total[:, b * CP:b * CP + C]

    def send_half(u):
        for s in range(u * PLANE, (u + 1) * PLANE):
            gb[s, 0:R, :] = g32[s * R:(s + 1) * R, :]
            gb[s, R:RP, :] = jnp.zeros((RP - R, C), F32)
        src = gb.at[pl.ds(u * PLANE, PLANE), pl.ds(pl.multiple_of((1 - half) * H, 16), H), :]
        send(src, pr.at[pl.ds(u * PLANE, PLANE)], p_send.at[u], p_recv.at[u], (mate, me))

    done = 0
    lines = list(range(1, LN))
    for a in range(3):
        tap_rows(a)
        while done < LN and (done + 1) * PLANE * R <= (a + 1) * 3 * C:
            send_half(done)
            done += 1
        for dq in lines[a * len(lines) // 3:(a + 1) * len(lines) // 3]:
            pass_line(dq)

    shifted(x_ref, xc, 1)

    for u in range(LN):
        arrived(pr.at[pl.ds(u * PLANE, PLANE)], p_recv.at[u])
    mine = pl.ds(pl.multiple_of(half * H, 16), H)
    cols = [(px, 0), (py, 1), (pd, 2)]
    for dq in list(range(1, LN)) + [0]:
        for col, k in cols:
            s = shard_at(dq, col)
            sb[k, dq] = (gb[s, mine, :] + pr[s]).astype(BF16)
            send(sb.at[k, dq], r1.at[k, dq], a_send.at[k, dq], a_recv.at[k, dq], (grp, shard_at(0, col)))

    for dq in range(LN):
        pass_plane(dq)
    for dq in range(LN):
        wait_piece(shard_at(dq, pd))

    for s in range(S):
        w32[s * R:(s + 1) * R, :] = wg[s].astype(F32)[0:R]
    for t in range(9):
        a, b = t // 3, t % 3
        tap = w32[t * C:(t + 1) * C, :]
        wf[a, b * CP:b * CP + C, :] = tap.astype(BF16)
        wb[a, b * CP:b * CP + C, :] = tap.T.astype(BF16)
        for dst in (wf, wb):
            dst[a, b * CP + C:(b + 1) * CP, :] = jnp.zeros((CP - C, C), BF16)

    outs = []
    MT = cells // 2

    def conv(buf, ker, acc, out, sign, sem):
        for img in range(images):
            for part in range(cells // MT):
                row = part * MT
                val = None
                for a in range(3):
                    lo = WW + sign * WW * (a - 1) + row
                    term = jnp.dot(buf[img, lo:lo + MT, :], ker[a], preferred_element_type=F32)
                    val = term if val is None else val + term
                at = img * cells + row
                acc[at:at + MT, :] = val
                copy = pltpu.make_async_copy(acc.at[pl.ds(at, MT)], out.at[pl.ds(at, MT)],
                                             out_sem.at[sem, img * (cells // MT) + part])
                copy.start()
                outs.append(copy)

    conv(xc, wf, acc_a, act_ref, 1, 0)

    def plane_sum(dq):
        s = shard_at(dq, p)
        total = gb[s, mine, :] + pr[s]
        for k in range(3):
            arrived(r1.at[k, dq], a_recv.at[k, dq])
            total = total + r1[k, dq].astype(F32)
        return total

    for dq in range(1, LN):
        s2[dq - 1] = plane_sum(dq).astype(BF16)
        send(s2.at[dq - 1], r2.at[dq - 1], b_send.at[dq - 1], b_recv.at[dq - 1], (grp, shard_at(dq, p)))
    keep[...] = plane_sum(0)

    conv(gc, wb, acc_d, dg_ref, -1, 1)

    total = keep[...]
    for k in range(LN - 1):
        arrived(r2.at[k], b_recv.at[k])
        total = total + r2[k].astype(F32)
    tot[mine, :] = total
    send(tot.at[mine], tot.at[mine], t_send, t_recv, (mate, me))
    arrived(pw, e_recv.at[0])
    arrived(pm, e_recv.at[1])
    other = pl.ds(pl.multiple_of((1 - half) * H, 16), H)
    arrived(tot.at[other], t_recv)
    cells_group = S * images * cells
    grad = tot[0:R, :] * (0.5 * float(cells_group) ** -0.5)
    rate = peak_rate * (step_ref[0] + 1).astype(F32) / warm_steps
    moment = 0.5 * beta_rate * (m_ref[...] + pm[...]) + grad
    nm_ref[...] = moment
    nw_ref[...] = 0.5 * (w_ref[...] + pw[...]) - rate * moment

    for copy in started:
        copy.wait_send()
    for copy in outs:
        copy.wait()


def run_step(latents, cotangent, weights, momentum, step, bit):
    S = lax.axis_size("shard")
    images, HH, WW, C = latents.shape
    R = weights.shape[1]
    RP = -(-R // 32) * 32
    H = RP // 2
    LN = S // PLANE
    cells = HH * WW
    CP = 384
    dims = (S, R, RP, C, images, HH, WW)
    vmem = pl.BlockSpec(memory_space=pltpu.VMEM)
    smem = pl.BlockSpec(memory_space=pltpu.SMEM)
    hbm = pl.BlockSpec(memory_space=pl.ANY)
    V = pltpu.VMEM
    dma = pltpu.SemaphoreType.DMA
    flat = images * cells
    scratch = [
        V((images, cells + 2 * WW, 3 * CP), BF16),
        V((images, cells + 2 * WW, 3 * CP), BF16),
        V((images, C, cells), BF16),
        V((S, RP, C), BF16),
        V((9 * C, C), F32),
        V((3, 3 * CP, C), BF16),
        V((3, 3 * CP, C), BF16),
        V((9 * C, C), F32),
        V((S, RP, C), F32),
        V((S, H, C), F32),
        V((H, C), F32),
        V((3, LN, H, C), BF16),
        V((3, LN, H, C), BF16),
        V((LN - 1, H, C), BF16),
        V((LN - 1, H, C), BF16),
        V((RP, C), F32),
        V((8, 128), F32),
        V((R, C), F32),
        V((R, C), F32),
        V((flat, C), F32),
        V((flat, C), F32),
        dma((4 * LN + 1,)), dma((S,)),
        dma((2,)), dma((2,)),
        dma((LN,)), dma((LN,)),
        dma((3, LN)), dma((3, LN)),
        dma((LN - 1,)), dma((LN - 1,)),
        dma, dma,
        dma((2, 2 * images)),
    ]
    flops = 6 * flat * 9 * C * C
    act, dg, nw, nm = pl.pallas_call(
        partial(step_kernel, bit, dims),
        out_shape=(
            jax.ShapeDtypeStruct((flat, C), F32),
            jax.ShapeDtypeStruct((flat, C), F32),
            jax.ShapeDtypeStruct((R, C), F32),
            jax.ShapeDtypeStruct((R, C), F32),
        ),
        in_specs=[vmem, vmem, vmem, vmem, smem],
        out_specs=(hbm, hbm, vmem, vmem),
        scratch_shapes=scratch,
        compiler_params=pltpu.CompilerParams(
            collective_id=bit, has_side_effects=True, vmem_limit_bytes=60 * 1024 * 1024),
        cost_estimate=pl.CostEstimate(flops=flops, bytes_accessed=12 * flat * C, transcendentals=0),
    )(latents.reshape(flat, C), cotangent.reshape(flat, C), weights[0], momentum[0], step)
    return act.reshape(latents.shape), dg.reshape(latents.shape), nw[None], nm[None]


def shards(latents, cotangent, weights, momentum, step):
    bit_count = lax.axis_size("group").bit_length() - 1
    branches = [partial(run_step, bit=bit) for bit in range(bit_count)]
    args = (latents, cotangent, weights, momentum, step)
    if bit_count == 1:
        return branches[0](*args)
    return lax.switch(step[0] % bit_count, branches, *args)


def solution(mesh):
    placed = (
        P(("group", "shard"), None, None, None),
        P(("group", "shard"), None, None, None),
        P("group", "shard", None),
        P("group", "shard", None),
        P(),
    )
    return jax.shard_map(
        shards,
        mesh=mesh,
        in_specs=placed,
        out_specs=(
            P(("group", "shard"), None, None, None),
            P(("group", "shard"), None, None, None),
            P("group", "shard", None),
            P("group", "shard", None),
        ),
        check_vma=False,
    )
```

time: 261 us -> 81.7 us (0.31)
  the two profiles are of different devices: /device:TPU:0 before, /device:TPU:11 now
where the time goes in v1:
time: 81.7 us; the launch traced here: 81.5 us
  Pallas kernels  68.9 us (84%)
  local copies, waits for them, and re-layouts  11.4 us (14%)
  between operations  1.29 us (2%)
    pallas_call x1, Pallas kernels, run_step(): pl.pallas_call(partial(step_kernel, bit, dims), out_shape=(jax.ShapeDtype...  68.9 us
    unnamed x7, local copies, waits for them, and re-layouts  11.4 us

profile of v1, /device:TPU:11, one launch (start us, length us, event | category | flops | bytes accessed | tf_op | source)
XLA Modules:
  0.0 81.5 jit_solution(14729299130512672851)
XLA Ops:
  1.3 1.9 %copy_bitcast_fusion = (f32[180,320]{1,0:T(8,128)}, f32[180,320]{1,0:T(8,128)}) fusion(f32[1,180,320]{2,0,1:T(1,128)} %param.8, f32[1,180,320]{2,0,1:T(1,128)} %param.7), kind=kLoop, calls=%fused_computation | loop fusion | bytes 921600
  3.2 68.9 %shard_map.84 = (f32[2048,320]{1,0:T(8,128)}, f32[2048,320]{1,0:T(8,128)}, f32[180,320]{1,0:T(8,128)}, f32[180,320]{1,0:T(8,128)}) custom-call(bf16[2048,320]{1,0:T(8,128)(2,1)} %bitcast.14, bf16[2048,320]{1,0:T(8,128)(2,1)} %bitcast.15, f32[180,320]{1,0:T(8,128)} %get-tuple-element.17.w_ref, f32[180,320]{1,0:T(8,128)} %get-tuple-element.16.m_ref, ...), custom_call_target="tpu_custom_call" | custom-call | flops 11324620800 | bytes 7864320 | tf_op jit(solution)/shard_map/pallas_call | solution.py:288
  72.0 1.9 %copy.9 = f32[1,180,320]{2,0,1:T(1,128)} copy(f32[1,180,320]{2,1,0:T(8,128)} %bitcast.13) | data formatting | bytes 460800
  74.0 1.9 %copy.10 = f32[1,180,320]{2,0,1:T(1,128)} copy(f32[1,180,320]{2,1,0:T(8,128)} %bitcast.12) | data formatting | bytes 460800
  75.9 0.0 copy-start
  75.9 3.9 %copy.18 = f32[2,32,32,320]{3,2,1,0:T(8,128)} copy(f32[2,32,32,320]{3,2,1,0:T(8,128)} %bitcast.11) | data formatting | bytes 5242880
  79.8 0.0 copy-done
  79.8 1.7 %copy.19 = f32[2,32,32,320]{3,2,1,0:T(8,128)} copy(f32[2,32,32,320]{3,2,1,0:T(8,128)S(1)} %bitcast.10) | data formatting | bytes 5242880
Async XLA Ops:
  75.9 3.9 %copy-start = (f32[2048,320]{1,0:T(8,128)S(1)}, f32[2048,320]{1,0:T(8,128)}, u32[]{:S(2)}) copy-start(f32[2048,320]{1,0:T(8,128)} %get-tuple-element.9) | copy-start | bytes 7864324

commit v2 on v1

v2 whole, which is shorter than its diff:
```python
from functools import partial

import jax
import jax.numpy as jnp
from jax import lax
from jax.experimental import pallas as pl
from jax.experimental.pallas import tpu as pltpu
from jax.sharding import PartitionSpec as P

beta_rate = 0.9
peak_rate = 0.1
warm_steps = 64.0
MESH = pl.DeviceIdType.MESH
F32 = jnp.float32
BF16 = jnp.bfloat16
PLANE = 4


def pack(rows):
    n, width = rows.shape
    full = width // 128
    parts = [rows[:, 128 * k:128 * (k + 1)] for k in range(full)]
    tail = rows[:, 128 * full:]
    return jnp.concatenate(parts + [jnp.concatenate([tail[:n // 2], tail[n // 2:]], 1)], 0)


def unpack(packed, n):
    full = (packed.shape[0] - n // 2) // n
    parts = [packed[n * k:n * (k + 1)] for k in range(full)]
    tail = packed[n * full:]
    return jnp.concatenate(parts + [jnp.concatenate([tail[:, :64], tail[:, 64:]], 0)], 1)


def step_kernel(bit, dims, x_hbm, c_hbm, w_ref, m_ref, step_ref,
                act_ref, dg_ref, nw_ref, nm_ref,
                x_ref, c_ref, xc, gc, xt, wg, w32, wf, wb, g32, gb, pr, keep, sb, r1, s2, r2, tot,
                pw, pm, wide, acc_a, acc_d,
                g_send, g_recv, e_send, e_recv, p_send, p_recv, a_send, a_recv,
                b_send, b_recv, t_send, t_recv, in_sem, out_sem):
    S, R, RP, C, images, HH, WW = dims
    H = RP // 2
    LN = S // PLANE
    cells = HH * WW
    grp = lax.axis_index("group")
    me = lax.axis_index("shard")
    q = me // PLANE
    p = me % PLANE
    px = p + 1 - 2 * (p % 2)
    py = (p + 2) % PLANE
    pd = PLANE - 1 - p
    mask = 2 ** bit
    half = (grp // mask) % 2
    mate = grp + mask - 2 * mask * half

    def shard_at(dq, col):
        return ((q + dq) % LN) * PLANE + col

    barrier = pltpu.get_barrier_semaphore()
    peers = [(grp, shard_at(dq, p)) for dq in range(1, LN)]
    peers += [(grp, shard_at(0, col)) for col in (px, py, pd)]
    peers += [(mate, me)]
    for peer in peers:
        pl.semaphore_signal(barrier, inc=1, device_id=peer, device_id_type=MESH)

    in_x = pltpu.make_async_copy(x_hbm, x_ref, in_sem.at[0])
    in_c = pltpu.make_async_copy(c_hbm, c_ref, in_sem.at[1])
    in_c.start()
    in_x.start()
    own = w_ref[:, 0, :]
    wg[me, 0] = pack(own[0:H]).astype(BF16)
    wg[me, 1] = pack(jnp.concatenate([own[H:R], jnp.zeros((RP - R, C), F32)], 0)).astype(BF16)
    pl.semaphore_wait(barrier, len(peers))

    started = []

    def send(src, dst, ss, rs, peer):
        copy = pltpu.make_async_remote_copy(src_ref=src, dst_ref=dst, send_sem=ss, recv_sem=rs,
                                            device_id=peer, device_id_type=MESH)
        copy.start()
        started.append(copy)

    def arrived(ref, sem):
        pltpu.make_async_copy(ref, ref, sem).wait()

    g_count = [0]

    def send_piece(slot, peer):
        send(wg.at[slot], wg.at[slot], g_send.at[g_count[0]], g_recv.at[slot], peer)
        g_count[0] += 1

    def wait_piece(slot):
        arrived(wg.at[slot], g_recv.at[slot])

    for dq in range(1, LN):
        send_piece(me, (grp, shard_at(dq, p)))
    x_peer = (grp, shard_at(0, px))
    y_peer = (grp, shard_at(0, py))
    send_piece(me, x_peer)
    send_piece(me, y_peer)
    send(w_ref, pw, e_send.at[0], e_recv.at[0], (mate, me))
    send(m_ref, pm, e_send.at[1], e_recv.at[1], (mate, me))

    def pass_line(dq):
        slot = shard_at(dq, p)
        wait_piece(slot)
        send_piece(slot, x_peer)
        send_piece(slot, y_peer)

    def pass_plane(dq):
        slot_x = shard_at(dq, px)
        slot_y = shard_at(dq, py)
        wait_piece(slot_x)
        wait_piece(slot_y)
        if dq % 2 == 0:
            send_piece(slot_x, y_peer)
        else:
            send_piece(slot_y, x_peer)

    CH = 8 * WW
    for buf in (xc, gc):
        for img in range(images):
            buf[img, 0:WW, :] = jnp.zeros((WW, 3 * C), BF16)
            buf[img, WW + cells:, :] = jnp.zeros((WW, 3 * C), BF16)

    def shifted(src, buf, sign):
        def body(k, _):
            img = k // (cells // CH)
            row = (k % (cells // CH)) * CH
            mid = src[pl.ds(pl.multiple_of(k * CH, CH), CH), :]
            val = mid.astype(F32)
            col = lax.broadcasted_iota(jnp.int32, (CH, C), 0) % WW
            prev = jnp.where(col == 0, 0.0, pltpu.roll(val, 1, 0)).astype(BF16)
            nxt = jnp.where(col == WW - 1, 0.0, pltpu.roll(val, CH - 1, 0)).astype(BF16)
            first, last = (prev, nxt) if sign > 0 else (nxt, prev)
            dst = pl.ds(pl.multiple_of(WW + row, WW), CH)
            buf[img, dst, :] = jnp.concatenate([first, mid, last], 1)
            return 0
        lax.fori_loop(0, images * (cells // CH), body, 0)

    in_c.wait()
    shifted(c_ref, gc, -1)
    in_x.wait()
    for img in range(images):
        xt[img] = x_ref[img * cells:(img + 1) * cells, :].T
    pass_plane(0)

    def tap_rows(a):
        total = None
        for img in range(images):
            part = jnp.dot(xt[img], gc[img, WW - WW * (a - 1):WW - WW * (a - 1) + cells, :],
                           preferred_element_type=F32)
            total = part if total is None else total + part
        for b in range(3):
            t = 3 * a + b
            g32[t * C:(t + 1) * C, :] = total[:, b * C:(b + 1) * C]

    def send_half(u):
        for s in range(u * PLANE, (u + 1) * PLANE):
            gb[s, 0] = pack(g32[s * R:s * R + H, :])
            gb[s, 1] = pack(jnp.concatenate([g32[s * R + H:(s + 1) * R, :], jnp.zeros((RP - R, C), F32)], 0))
        group = pl.ds(u * PLANE, PLANE)
        send(gb.at[group, 1 - half], pr.at[group], p_send.at[u], p_recv.at[u], (mate, me))

    done = 0
    lines = list(range(1, LN))
    planes = list(range(1, LN))
    for a in range(3):
        tap_rows(a)
        while done < LN and (done + 1) * PLANE * R <= (a + 1) * 3 * C:
            send_half(done)
            done += 1
        for dq in lines[a * len(lines) // 3:(a + 1) * len(lines) // 3]:
            pass_line(dq)
        for dq in planes[max(a - 1, 0) * len(planes) // 3:a * len(planes) // 3]:
            pass_plane(dq)

    shifted(x_ref, xc, 1)

    for u in range(LN):
        arrived(pr.at[pl.ds(u * PLANE, PLANE)], p_recv.at[u])
    cols = [(px, 0), (py, 1), (pd, 2)]
    for dq in list(range(1, LN)) + [0]:
        for col, k in cols:
            s = shard_at(dq, col)
            sb[k, dq] = (gb[s, half] + pr[s]).astype(BF16)
            send(sb.at[k, dq], r1.at[k, dq], a_send.at[k, dq], a_recv.at[k, dq], (grp, shard_at(0, col)))

    for dq in planes[2 * len(planes) // 3:]:
        pass_plane(dq)
    for dq in range(LN):
        wait_piece(shard_at(dq, pd))

    for s in range(S):
        w32[s * R:s * R + H, :] = unpack(wg[s, 0].astype(F32), H)
        w32[s * R + H:(s + 1) * R, :] = unpack(wg[s, 1].astype(F32), H)[0:R - H]
    for a in range(3):
        wf[:, a * C:(a + 1) * C] = w32[3 * a * C:3 * (a + 1) * C, :].astype(BF16)
    for b in range(3):
        wb[b * C:(b + 1) * C, :] = jnp.concatenate(
            [w32[(3 * a + b) * C:(3 * a + b + 1) * C, :].astype(BF16).T for a in range(3)], 1)

    outs = []

    def conv(buf, ker, acc, out, sign, sem):
        for img in range(images):
            wide[...] = jnp.dot(buf[img], ker[...], preferred_element_type=F32)
            val = None
            for a in range(3):
                lo = WW + sign * WW * (a - 1)
                term = wide[lo:lo + cells, a * C:(a + 1) * C]
                val = term if val is None else val + term
            rows = pl.ds(img * cells, cells)
            acc[rows, :] = val
            copy = pltpu.make_async_copy(acc.at[rows], out.at[rows], out_sem.at[sem, img])
            copy.start()
            outs.append(copy)

    conv(xc, wf, acc_a, act_ref, 1, 0)

    def plane_sum(dq):
        s = shard_at(dq, p)
        total = gb[s, half] + pr[s]
        for k in range(3):
            arrived(r1.at[k, dq], a_recv.at[k, dq])
            total = total + r1[k, dq].astype(F32)
        return total

    for dq in range(1, LN):
        s2[dq - 1] = plane_sum(dq).astype(BF16)
        send(s2.at[dq - 1], r2.at[dq - 1], b_send.at[dq - 1], b_recv.at[dq - 1], (grp, shard_at(dq, p)))
    keep[...] = plane_sum(0)

    conv(gc, wb, acc_d, dg_ref, -1, 1)

    total = keep[...]
    for k in range(LN - 1):
        arrived(r2.at[k], b_recv.at[k])
        total = total + r2[k].astype(F32)
    tot[half] = total
    send(tot.at[half], tot.at[half], t_send, t_recv, (mate, me))
    arrived(pw, e_recv.at[0])
    arrived(pm, e_recv.at[1])
    arrived(tot.at[1 - half], t_recv)
    cells_group = S * images * cells
    rows = jnp.concatenate([unpack(tot[0], H), unpack(tot[1], H)[0:R - H]], 0)
    grad = rows * (0.5 * float(cells_group) ** -0.5)
    rate = peak_rate * (step_ref[0] + 1).astype(F32) / warm_steps
    moment = 0.5 * beta_rate * (m_ref[:, 0, :] + pm[:, 0, :]) + grad
    nm_ref[:, 0, :] = moment
    nw_ref[:, 0, :] = 0.5 * (w_ref[:, 0, :] + pw[:, 0, :]) - rate * moment

    for copy in started:
        copy.wait_send()
    for copy in outs:
        copy.wait()


def run_step(latents, cotangent, weights, momentum, step, bit):
    S = lax.axis_size("shard")
    images, HH, WW, C = latents.shape
    R = weights.shape[1]
    RP = -(-R // 64) * 64
    H = RP // 2
    LN = S // PLANE
    cells = HH * WW
    PK = H * C // 128
    dims = (S, R, RP, C, images, HH, WW)
    vmem = pl.BlockSpec(memory_space=pltpu.VMEM)
    smem = pl.BlockSpec(memory_space=pltpu.SMEM)
    hbm = pl.BlockSpec(memory_space=pl.ANY)
    V = pltpu.VMEM
    dma = pltpu.SemaphoreType.DMA
    flat = images * cells
    scratch = [
        V((flat, C), BF16),
        V((flat, C), BF16),
        V((images, cells + 2 * WW, 3 * C), BF16),
        V((images, cells + 2 * WW, 3 * C), BF16),
        V((images, C, cells), BF16),
        V((S, 2, PK, 128), BF16),
        V((9 * C, C), F32),
        V((3 * C, 3 * C), BF16),
        V((3 * C, 3 * C), BF16),
        V((9 * C, C), F32),
        V((S, 2, PK, 128), F32),
        V((S, PK, 128), F32),
        V((PK, 128), F32),
        V((3, LN, PK, 128), BF16),
        V((3, LN, PK, 128), BF16),
        V((LN - 1, PK, 128), BF16),
        V((LN - 1, PK, 128), BF16),
        V((2, PK, 128), F32),
        V((R, 1, C), F32),
        V((R, 1, C), F32),
        V((cells + 2 * WW, 3 * C), F32),
        V((flat, C), F32),
        V((flat, C), F32),
        dma((4 * LN + 1,)), dma((S,)),
        dma((2,)), dma((2,)),
        dma((LN,)), dma((LN,)),
        dma((3, LN)), dma((3, LN)),
        dma((LN - 1,)), dma((LN - 1,)),
        dma, dma,
        dma((2,)),
        dma((2, images)),
    ]
    flops = 6 * flat * 9 * C * C
    act, dg, nw, nm = pl.pallas_call(
        partial(step_kernel, bit, dims),
        out_shape=(
            jax.ShapeDtypeStruct((flat, C), F32),
            jax.ShapeDtypeStruct((flat, C), F32),
            jax.ShapeDtypeStruct((R, 1, C), F32),
            jax.ShapeDtypeStruct((R, 1, C), F32),
        ),
        in_specs=[hbm, hbm, vmem, vmem, smem],
        out_specs=(hbm, hbm, vmem, vmem),
        scratch_shapes=scratch,
        compiler_params=pltpu.CompilerParams(
            collective_id=bit, has_side_effects=True, vmem_limit_bytes=60 * 1024 * 1024),
        cost_estimate=pl.CostEstimate(flops=flops, bytes_accessed=12 * flat * C, transcendentals=0),
    )(latents.reshape(flat, C), cotangent.reshape(flat, C), weights.transpose(1, 0, 2), momentum.transpose(1, 0, 2), step)
    return act.reshape(latents.shape), dg.reshape(latents.shape), nw.transpose(1, 0, 2), nm.transpose(1, 0, 2)


def shards(latents, cotangent, weights, momentum, step):
    bit_count = lax.axis_size("group").bit_length() - 1
    branches = [partial(run_step, bit=bit) for bit in range(bit_count)]
    args = (latents, cotangent, weights, momentum, step)
    if bit_count == 1:
        return branches[0](*args)
    return lax.switch(step[0] % bit_count, branches, *args)


def solution(mesh):
    placed = (
        P(("group", "shard"), None, None, None),
        P(("group", "shard"), None, None, None),
        P("group", "shard", None),
        P("group", "shard", None),
        P(),
    )
    return jax.shard_map(
        shards,
        mesh=mesh,
        in_specs=placed,
        out_specs=(
            P(("group", "shard"), None, None, None),
            P(("group", "shard"), None, None, None),
            P("group", "shard", None),
            P("group", "shard", None),
        ),
        check_vma=False,
    )
```

time: 81.7 us -> 64.4 us (0.79)
  the two profiles are of different devices: /device:TPU:11 before, /device:TPU:0 now
where the time goes in v2:
time: 64.4 us; the launch traced here: 64.2 us
  Pallas kernels  55.9 us (87%)
  local copies, waits for them, and re-layouts  7 us (11%)
  between operations  1.3 us (2%)
    pallas_call x1, Pallas kernels, run_step(): pl.pallas_call(partial(step_kernel, bit, dims), out_shape=(jax.ShapeDtype...  55.9 us
    unnamed x10, local copies, waits for them, and re-layouts  7 us

profile of v2, /device:TPU:0, one launch (start us, length us, event | category | flops | bytes accessed | tf_op | source)
XLA Modules:
  0.0 64.2 jit_solution(13792564359643710532)
XLA Ops:
  1.3 55.9 %shard_map.84 = (f32[2048,320]{1,0:T(8,128)}, f32[2048,320]{1,0:T(8,128)}, f32[180,1,320]{2,1,0:T(1,128)}, f32[180,1,320]{2,1,0:T(1,128)}) custom-call(bf16[2048,320]{1,0:T(8,128)(2,1)} %bitcast.12, bf16[2048,320]{1,0:T(8,128)(2,1)} %bitcast.13, f32[180,1,320]{2,1,0:T(1,128)} %bitcast.14, f32[180,1,320]{2,1,0:T(1,128)} %bitcast.15, s32[1]{0:T(128)S(6)} %copy.13.step_ref), custom_call_target="tpu_custom_call" | custom-call | flops 11324620800 | bytes 7864320 | tf_op jit(solution)/shard_map/pallas_call | solution.py:308
  57.2 0.0 copy-start
  57.2 3.9 %copy.14 = f32[2,32,32,320]{3,2,1,0:T(8,128)} copy(f32[2,32,32,320]{3,2,1,0:T(8,128)} %bitcast.9) | data formatting | bytes 5242880
  61.1 0.0 copy-done
  61.2 0.0 copy-start.2
  61.2 0.0 copy-start.1
  61.2 1.7 %copy.15 = f32[2,32,32,320]{3,2,1,0:T(8,128)} copy(f32[2,32,32,320]{3,2,1,0:T(8,128)S(1)} %bitcast.8) | data formatting | bytes 5242880
  62.8 0.0 copy-done.2
  62.8 0.7 %copy.16 = f32[1,180,320]{2,0,1:T(1,128)} copy(f32[1,180,320]{2,0,1:T(1,128)S(1)} %bitcast.11) | data formatting | bytes 460800
  63.5 0.0 copy-done.1
  63.5 0.7 %copy.17 = f32[1,180,320]{2,0,1:T(1,128)} copy(f32[1,180,320]{2,0,1:T(1,128)S(1)} %bitcast.10) | data formatting | bytes 460800
Async XLA Ops:
  57.2 3.9 %copy-start = (f32[2048,320]{1,0:T(8,128)S(1)}, f32[2048,320]{1,0:T(8,128)}, u32[]{:S(2)}) copy-start(f32[2048,320]{1,0:T(8,128)} %get-tuple-element.9) | copy-start | bytes 7864324
  61.2 1.7 %copy-start.2 = (f32[180,1,320]{2,1,0:T(1,128)S(1)}, f32[180,1,320]{2,1,0:T(1,128)}, u32[]{:S(2)}) copy-start(f32[180,1,320]{2,1,0:T(1,128)} %get-tuple-element.10) | copy-start | bytes 691204
  61.2 2.4 %copy-start.1 = (f32[180,1,320]{2,1,0:T(1,128)S(1)}, f32[180,1,320]{2,1,0:T(1,128)}, u32[]{:S(2)}) copy-start(f32[180,1,320]{2,1,0:T(1,128)} %get-tuple-element.11) | copy-start | bytes 691204

commit v3 on v2

--- a/solution.py
+++ b/solution.py
@@ -33,8 +33,8 @@
 
 def step_kernel(bit, dims, x_hbm, c_hbm, w_ref, m_ref, step_ref,
                 act_ref, dg_ref, nw_ref, nm_ref,
-                x_ref, c_ref, xc, gc, xt, wg, w32, wf, wb, g32, gb, pr, keep, sb, r1, s2, r2, tot,
-                pw, pm, wide, acc_a, acc_d,
+                x_ref, c_ref, xc, gc, xt, wg, wf, wb, g32, gb, pr, keep, sb, r1, s2, r2, tot,
+                pw, pm, wide, acc,
                 g_send, g_recv, e_send, e_recv, p_send, p_recv, a_send, a_recv,
                 b_send, b_recv, t_send, t_recv, in_sem, out_sem):
     S, R, RP, C, images, HH, WW = dims
@@ -142,7 +142,23 @@
     in_x.wait()
     for img in range(images):
         xt[img] = x_ref[img * cells:(img + 1) * cells, :].T
-    pass_plane(0)
+
+    order = []
+    for dq in range(1, LN // 2 + 1):
+        order += [dq, LN - dq] if 2 * dq != LN else [dq]
+    tasks = [partial(pass_line, order[0]), partial(pass_plane, 0)]
+    tasks += [partial(pass_line, dq) for dq in order[1:]]
+    tasks += [partial(pass_plane, dq) for dq in order]
+    points = 3 * images + 1
+    turn = [0]
+
+    def pass_on():
+        lo, hi = turn[0] * len(tasks) // points, (turn[0] + 1) * len(tasks) // points
+        for task in tasks[lo:hi]:
+            task()
+        turn[0] += 1
+
+    pass_on()
 
     def tap_rows(a):
         total = None
@@ -150,6 +166,7 @@
             part = jnp.dot(xt[img], gc[img, WW - WW * (a - 1):WW - WW * (a - 1) + cells, :],
                            preferred_element_type=F32)
             total = part if total is None else total + part
+            pass_on()
         for b in range(3):
             t = 3 * a + b
             g32[t * C:(t + 1) * C, :] = total[:, b * C:(b + 1) * C]
@@ -161,76 +178,77 @@
         group = pl.ds(u * PLANE, PLANE)
         send(gb.at[group, 1 - half], pr.at[group], p_send.at[u], p_recv.at[u], (mate, me))
 
+    cols = [(px, 0), (py, 1), (pd, 2)]
+
+    def send_plane(u):
+        arrived(pr.at[pl.ds(u * PLANE, PLANE)], p_recv.at[u])
+        for col, k in cols:
+            sb[k, u] = (gb[u * PLANE + col, half] + pr[u * PLANE + col]).astype(BF16)
+            send(sb.at[k, u], r1.at[k, u], a_send.at[k, u], a_recv.at[k, u], (grp, shard_at(0, col)))
+
     done = 0
-    lines = list(range(1, LN))
-    planes = list(range(1, LN))
+    sent = 0
     for a in range(3):
         tap_rows(a)
+        ready = done
         while done < LN and (done + 1) * PLANE * R <= (a + 1) * 3 * C:
             send_half(done)
             done += 1
-        for dq in lines[a * len(lines) // 3:(a + 1) * len(lines) // 3]:
-            pass_line(dq)
-        for dq in planes[max(a - 1, 0) * len(planes) // 3:a * len(planes) // 3]:
-            pass_plane(dq)
+        while sent < ready:
+            send_plane(sent)
+            sent += 1
 
     shifted(x_ref, xc, 1)
-
-    for u in range(LN):
-        arrived(pr.at[pl.ds(u * PLANE, PLANE)], p_recv.at[u])
-    cols = [(px, 0), (py, 1), (pd, 2)]
-    for dq in list(range(1, LN)) + [0]:
-        for col, k in cols:
-            s = shard_at(dq, col)
-            sb[k, dq] = (gb[s, half] + pr[s]).astype(BF16)
-            send(sb.at[k, dq], r1.at[k, dq], a_send.at[k, dq], a_recv.at[k, dq], (grp, shard_at(0, col)))
-
-    for dq in planes[2 * len(planes) // 3:]:
-        pass_plane(dq)
+    while sent < LN:
+        send_plane(sent)
+        sent += 1
     for dq in range(LN):
         wait_piece(shard_at(dq, pd))
 
     for s in range(S):
-        w32[s * R:s * R + H, :] = unpack(wg[s, 0].astype(F32), H)
-        w32[s * R + H:(s + 1) * R, :] = unpack(wg[s, 1].astype(F32), H)[0:R - H]
+        g32[s * R:s * R + H, :] = unpack(wg[s, 0].astype(F32), H)
+        g32[s * R + H:(s + 1) * R, :] = unpack(wg[s, 1].astype(F32), H)[0:R - H]
     for a in range(3):
-        wf[:, a * C:(a + 1) * C] = w32[3 * a * C:3 * (a + 1) * C, :].astype(BF16)
+        wf[:, a * C:(a + 1) * C] = g32[3 * a * C:3 * (a + 1) * C, :].astype(BF16)
+
+    outs = {}
+
+    def conv(buf, ker, out, sign, sem, img):
+        wide[...] = jnp.dot(buf[img], ker[...], preferred_element_type=F32)
+        val = None
+        for a in range(3):
+            lo = WW + sign * WW * (a - 1)
+            term = wide[lo:lo + cells, a * C:(a + 1) * C]
+            val = term if val is None else val + term
+        rows = pl.ds(img * cells, cells)
+        if img in outs:
+            outs.pop(img).wait()
+        acc[rows, :] = val
+        outs[img] = pltpu.make_async_copy(acc.at[rows], out.at[rows], out_sem.at[sem, img])
+        outs[img].start()
+
+    def plane_sum(dq):
+        u = (q + dq) % LN
+        total = gb[u * PLANE + p, half] + pr[u * PLANE + p]
+        for k in range(3):
+            arrived(r1.at[k, u], a_recv.at[k, u])
+            total = total + r1[k, u].astype(F32)
+        return total
+
+    def send_line(dq):
+        s2[dq - 1] = plane_sum(dq).astype(BF16)
+        send(s2.at[dq - 1], r2.at[dq - 1], b_send.at[dq - 1], b_recv.at[dq - 1], (grp, shard_at(dq, p)))
+
+    for img in range(images):
+        conv(xc, wf, act_ref, 1, 0, img)
     for b in range(3):
         wb[b * C:(b + 1) * C, :] = jnp.concatenate(
-            [w32[(3 * a + b) * C:(3 * a + b + 1) * C, :].astype(BF16).T for a in range(3)], 1)
-
-    outs = []
-
-    def conv(buf, ker, acc, out, sign, sem):
-        for img in range(images):
-            wide[...] = jnp.dot(buf[img], ker[...], preferred_element_type=F32)
-            val = None
-            for a in range(3):
-                lo = WW + sign * WW * (a - 1)
-                term = wide[lo:lo + cells, a * C:(a + 1) * C]
-                val = term if val is None else val + term
-            rows = pl.ds(img * cells, cells)
-            acc[rows, :] = val
-            copy = pltpu.make_async_copy(acc.at[rows], out.at[rows], out_sem.at[sem, img])
-            copy.start()
-            outs.append(copy)
-
-    conv(xc, wf, acc_a, act_ref, 1, 0)
-
-    def plane_sum(dq):
-        s = shard_at(dq, p)
-        total = gb[s, half] + pr[s]
-        for k in range(3):
-            arrived(r1.at[k, dq], a_recv.at[k, dq])
-            total = total + r1[k, dq].astype(F32)
-        return total
-
+            [g32[(3 * a + b) * C:(3 * a + b + 1) * C, :].astype(BF16).T for a in range(3)], 1)
     for dq in range(1, LN):
-        s2[dq - 1] = plane_sum(dq).astype(BF16)
-        send(s2.at[dq - 1], r2.at[dq - 1], b_send.at[dq - 1], b_recv.at[dq - 1], (grp, shard_at(dq, p)))
+        send_line(dq)
     keep[...] = plane_sum(0)
-
-    conv(gc, wb, acc_d, dg_ref, -1, 1)
+    for img in range(images - 1):
+        conv(gc, wb, dg_ref, -1, 1, img)
 
     total = keep[...]
     for k in range(LN - 1):
@@ -238,6 +256,7 @@
         total = total + r2[k].astype(F32)
     tot[half] = total
     send(tot.at[half], tot.at[half], t_send, t_recv, (mate, me))
+    conv(gc, wb, dg_ref, -1, 1, images - 1)
     arrived(pw, e_recv.at[0])
     arrived(pm, e_recv.at[1])
     arrived(tot.at[1 - half], t_recv)
@@ -251,7 +270,7 @@
 
     for copy in started:
         copy.wait_send()
-    for copy in outs:
+    for copy in outs.values():
         copy.wait()
 
 
@@ -278,7 +297,6 @@
         V((images, cells + 2 * WW, 3 * C), BF16),
         V((images, C, cells), BF16),
         V((S, 2, PK, 128), BF16),
-        V((9 * C, C), F32),
         V((3 * C, 3 * C), BF16),
         V((3 * C, 3 * C), BF16),
         V((9 * C, C), F32),
@@ -293,7 +311,6 @@
         V((R, 1, C), F32),
         V((R, 1, C), F32),
         V((cells + 2 * WW, 3 * C), F32),
-        V((flat, C), F32),
         V((flat, C), F32),
         dma((4 * LN + 1,)), dma((S,)),
         dma((2,)), dma((2,)),

time: 64.4 us -> 60.9 us (0.946)
  Pallas kernels: 55.9 us -> 52.4 us
    pallas_call x1, Pallas kernels: 55.9 us -> 52.4 us  [run_step(): pl.pallas_call(partial(step_kernel, bit, dims), out_shape=(jax.ShapeDtype...]
where the time goes in v3:
time: 60.9 us; the launch traced here: 60.7 us
  Pallas kernels  52.4 us (86%)
  local copies, waits for them, and re-layouts  7 us (11%)
  between operations  1.3 us (2%)
    pallas_call x1, Pallas kernels, run_step(): pl.pallas_call(partial(step_kernel, bit, dims), out_shape=(jax.ShapeDtype...  52.4 us
    unnamed x10, local copies, waits for them, and re-layouts  7 us

profile of v3, /device:TPU:0, one launch (start us, length us, event | category | flops | bytes accessed | tf_op | source)
XLA Modules:
  0.0 60.7 jit_solution(9152154005350013530)
XLA Ops:
  1.3 52.4 %shard_map.84 = (f32[2048,320]{1,0:T(8,128)}, f32[2048,320]{1,0:T(8,128)}, f32[180,1,320]{2,1,0:T(1,128)}, f32[180,1,320]{2,1,0:T(1,128)}) custom-call(bf16[2048,320]{1,0:T(8,128)(2,1)} %bitcast.12, bf16[2048,320]{1,0:T(8,128)(2,1)} %bitcast.13, f32[180,1,320]{2,1,0:T(1,128)} %bitcast.14, f32[180,1,320]{2,1,0:T(1,128)} %bitcast.15, s32[1]{0:T(128)S(6)} %copy.13.step_ref), custom_call_target="tpu_custom_call" | custom-call | flops 11324620800 | bytes 7864320 | tf_op jit(solution)/shard_map/pallas_call | solution.py:325
  53.7 0.0 copy-start
  53.7 3.9 %copy.14 = f32[2,32,32,320]{3,2,1,0:T(8,128)} copy(f32[2,32,32,320]{3,2,1,0:T(8,128)} %bitcast.9) | data formatting | bytes 5242880
  57.6 0.0 copy-done
  57.6 0.0 copy-start.2
  57.6 0.0 copy-start.1
  57.6 1.7 %copy.15 = f32[2,32,32,320]{3,2,1,0:T(8,128)} copy(f32[2,32,32,320]{3,2,1,0:T(8,128)S(1)} %bitcast.8) | data formatting | bytes 5242880
  59.3 0.0 copy-done.2
  59.3 0.7 %copy.16 = f32[1,180,320]{2,0,1:T(1,128)} copy(f32[1,180,320]{2,0,1:T(1,128)S(1)} %bitcast.11) | data formatting | bytes 460800
  60.0 0.0 copy-done.1
  60.0 0.7 %copy.17 = f32[1,180,320]{2,0,1:T(1,128)} copy(f32[1,180,320]{2,0,1:T(1,128)S(1)} %bitcast.10) | data formatting | bytes 460800
Async XLA Ops:
  53.7 3.9 %copy-start = (f32[2048,320]{1,0:T(8,128)S(1)}, f32[2048,320]{1,0:T(8,128)}, u32[]{:S(2)}) copy-start(f32[2048,320]{1,0:T(8,128)} %get-tuple-element.9) | copy-start | bytes 7864324
  57.6 1.7 %copy-start.2 = (f32[180,1,320]{2,1,0:T(1,128)S(1)}, f32[180,1,320]{2,1,0:T(1,128)}, u32[]{:S(2)}) copy-start(f32[180,1,320]{2,1,0:T(1,128)} %get-tuple-element.10) | copy-start | bytes 691204
  57.6 2.4 %copy-start.1 = (f32[180,1,320]{2,1,0:T(1,128)S(1)}, f32[180,1,320]{2,1,0:T(1,128)}, u32[]{:S(2)}) copy-start(f32[180,1,320]{2,1,0:T(1,128)} %get-tuple-element.11) | copy-start | bytes 691204

commit v4 on v3

--- a/solution.py
+++ b/solution.py
@@ -128,9 +128,11 @@
             row = (k % (cells // CH)) * CH
             mid = src[pl.ds(pl.multiple_of(k * CH, CH), CH), :]
             val = mid.astype(F32)
-            col = lax.broadcasted_iota(jnp.int32, (CH, C), 0) % WW
-            prev = jnp.where(col == 0, 0.0, pltpu.roll(val, 1, 0)).astype(BF16)
-            nxt = jnp.where(col == WW - 1, 0.0, pltpu.roll(val, CH - 1, 0)).astype(BF16)
+            col = lax.broadcasted_iota(jnp.int32, (1, WW, C), 1)
+            prev = pltpu.roll(val, 1, 0).reshape(CH // WW, WW, C)
+            prev = jnp.where(col == 0, 0.0, prev).reshape(CH, C).astype(BF16)
+            nxt = pltpu.roll(val, CH - 1, 0).reshape(CH // WW, WW, C)
+            nxt = jnp.where(col == WW - 1, 0.0, nxt).reshape(CH, C).astype(BF16)
             first, last = (prev, nxt) if sign > 0 else (nxt, prev)
             dst = pl.ds(pl.multiple_of(WW + row, WW), CH)
             buf[img, dst, :] = jnp.concatenate([first, mid, last], 1)
@@ -272,6 +274,41 @@
         copy.wait_send()
     for copy in outs.values():
         copy.wait()
+
+
+def relay_kernel(pieces, *refs):
+    count = (len(refs) - 2) // 3
+    srcs, dsts, holds = refs[:count], refs[count:2 * count], refs[2 * count:3 * count]
+    read_sem, write_sem = refs[3 * count:]
+    spans = []
+    for k in range(count):
+        step = srcs[k].shape[0] // pieces[k]
+        spans += [(k, pl.ds(i * step, step)) for i in range(pieces[k])]
+    reads = [pltpu.make_async_copy(srcs[k].at[at], holds[k].at[at], read_sem.at[i])
+             for i, (k, at) in enumerate(spans)]
+    writes = [pltpu.make_async_copy(holds[k].at[at], dsts[k].at[at], write_sem.at[i])
+              for i, (k, at) in enumerate(spans)]
+    for copy in reads:
+        copy.start()
+    for read, write in zip(reads, writes):
+        read.wait()
+        write.start()
+    for copy in writes:
+        copy.wait()
+
+
+def relay(arrays, pieces):
+    hbm = pl.BlockSpec(memory_space=pl.ANY)
+    total = sum(pieces)
+    return pl.pallas_call(
+        partial(relay_kernel, pieces),
+        out_shape=[jax.ShapeDtypeStruct(a.shape, a.dtype) for a in arrays],
+        in_specs=[hbm] * len(arrays),
+        out_specs=[hbm] * len(arrays),
+        scratch_shapes=[pltpu.VMEM(a.shape, a.dtype) for a in arrays]
+        + [pltpu.SemaphoreType.DMA((total,)), pltpu.SemaphoreType.DMA((total,))],
+        compiler_params=pltpu.CompilerParams(vmem_limit_bytes=60 * 1024 * 1024),
+    )(*arrays)
 
 
 def run_step(latents, cotangent, weights, momentum, step, bit):
@@ -337,6 +374,7 @@
             collective_id=bit, has_side_effects=True, vmem_limit_bytes=60 * 1024 * 1024),
         cost_estimate=pl.CostEstimate(flops=flops, bytes_accessed=12 * flat * C, transcendentals=0),
     )(latents.reshape(flat, C), cotangent.reshape(flat, C), weights.transpose(1, 0, 2), momentum.transpose(1, 0, 2), step)
+    act, dg, nw, nm = relay((act, dg, nw, nm), (4, 4, 1, 1))
     return act.reshape(latents.shape), dg.reshape(latents.shape), nw.transpose(1, 0, 2), nm.transpose(1, 0, 2)
 
 

time: 60.9 us -> 59.7 us (0.980)
  local copies, waits for them, and re-layouts: 7 us -> 0 us
  Pallas kernels: 52.4 us -> 58.1 us
    unnamed x10 -> x0, local copies, waits for them, and re-layouts: 7 us -> none
    pallas_call x0 -> x1, Pallas kernels: none -> 5.69 us  [relay(): pl.pallas_call(partial(relay_kernel, pieces), out_shape=[jax.ShapeDtypeSt...]
where the time goes in v4:
time: 59.7 us; the launch traced here: 59.6 us
  Pallas kernels  58.1 us (97%)
  between operations  1.45 us (2%)
    pallas_call x1, Pallas kernels, run_step(): pl.pallas_call(partial(step_kernel, bit, dims), out_shape=(jax.ShapeDtype...  52.4 us
    pallas_call x1, Pallas kernels, relay(): pl.pallas_call(partial(relay_kernel, pieces), out_shape=[jax.ShapeDtypeSt...  5.69 us

profile of v4, /device:TPU:0, one launch (start us, length us, event | category | flops | bytes accessed | tf_op | source)
XLA Modules:
  0.0 59.6 jit_solution(777793434700259128)
XLA Ops:
  1.3 52.4 %shard_map.84 = (f32[2048,320]{1,0:T(8,128)}, f32[2048,320]{1,0:T(8,128)}, f32[180,1,320]{2,1,0:T(1,128)}, f32[180,1,320]{2,1,0:T(1,128)}) custom-call(bf16[2048,320]{1,0:T(8,128)(2,1)} %bitcast.10, bf16[2048,320]{1,0:T(8,128)(2,1)} %bitcast.11, f32[180,1,320]{2,1,0:T(1,128)} %bitcast.12, f32[180,1,320]{2,1,0:T(1,128)} %bitcast.13, s32[1]{0:T(128)S(6)} %copy.9.step_ref), custom_call_target="tpu_custom_call" | custom-call | flops 11324620800 | bytes 7864320 | tf_op jit(solution)/shard_map/pallas_call | solution.py:362
  53.7 5.7 %shard_map.85 = (f32[2048,320]{1,0:T(8,128)}, f32[2048,320]{1,0:T(8,128)}, f32[180,1,320]{2,1,0:T(1,128)}, f32[180,1,320]{2,1,0:T(1,128)}) custom-call(f32[2048,320]{1,0:T(8,128)} %get-tuple-element.12.refs_0_, f32[2048,320]{1,0:T(8,128)} %get-tuple-element.13.refs_1_, f32[180,1,320]{2,1,0:T(1,128)} %get-tuple-element.14.refs_2_, ...), custom_call_target="tpu_custom_call" | custom-call | tf_op jit(solution)/shard_map/pallas_call | solution.py:303

commit v5 on v4

--- a/solution.py
+++ b/solution.py
@@ -139,12 +139,6 @@
             return 0
         lax.fori_loop(0, images * (cells // CH), body, 0)
 
-    in_c.wait()
-    shifted(c_ref, gc, -1)
-    in_x.wait()
-    for img in range(images):
-        xt[img] = x_ref[img * cells:(img + 1) * cells, :].T
-
     order = []
     for dq in range(1, LN // 2 + 1):
         order += [dq, LN - dq] if 2 * dq != LN else [dq]
@@ -160,7 +154,13 @@
             task()
         turn[0] += 1
 
+    in_c.wait()
+    shifted(c_ref, gc, -1)
+    in_x.wait()
     pass_on()
+    for img in range(images):
+        xt[img] = x_ref[img * cells:(img + 1) * cells, :].T
+        pass_on()
 
     def tap_rows(a):
         total = None

time: 59.7 us -> 59.7 us (level)
  no operation moved by 1% of the time
where the time goes in v5:
time: 59.7 us; the launch traced here: 59.6 us
  Pallas kernels  58.1 us (97%)
  between operations  1.45 us (2%)
    pallas_call x1, Pallas kernels, run_step(): pl.pallas_call(partial(step_kernel, bit, dims), out_shape=(jax.ShapeDtype...  52.4 us
    pallas_call x1, Pallas kernels, relay(): pl.pallas_call(partial(relay_kernel, pieces), out_shape=[jax.ShapeDtypeSt...  5.69 us

profile of v5, /device:TPU:0, one launch (start us, length us, event | category | flops | bytes accessed | tf_op | source)
XLA Modules:
  0.0 59.6 jit_solution(16939738184735530594)
XLA Ops:
  1.3 52.4 %shard_map.84 = (f32[2048,320]{1,0:T(8,128)}, f32[2048,320]{1,0:T(8,128)}, f32[180,1,320]{2,1,0:T(1,128)}, f32[180,1,320]{2,1,0:T(1,128)}) custom-call(bf16[2048,320]{1,0:T(8,128)(2,1)} %bitcast.10, bf16[2048,320]{1,0:T(8,128)(2,1)} %bitcast.11, f32[180,1,320]{2,1,0:T(1,128)} %bitcast.12, f32[180,1,320]{2,1,0:T(1,128)} %bitcast.13, s32[1]{0:T(128)S(6)} %copy.9.step_ref), custom_call_target="tpu_custom_call" | custom-call | flops 11324620800 | bytes 7864320 | tf_op jit(solution)/shard_map/pallas_call | solution.py:362
  53.7 5.7 %shard_map.85 = (f32[2048,320]{1,0:T(8,128)}, f32[2048,320]{1,0:T(8,128)}, f32[180,1,320]{2,1,0:T(1,128)}, f32[180,1,320]{2,1,0:T(1,128)}) custom-call(f32[2048,320]{1,0:T(8,128)} %get-tuple-element.12.refs_0_, f32[2048,320]{1,0:T(8,128)} %get-tuple-element.13.refs_1_, f32[180,1,320]{2,1,0:T(1,128)} %get-tuple-element.14.refs_2_, ...), custom_call_target="tpu_custom_call" | custom-call | tf_op jit(solution)/shard_map/pallas_call | solution.py:303
